TPU v7x, 32 devices: a whole 2x2x4 slice. The times are simulated.
32 devices in a mesh: row: 16 (over z, x, core), col: 2 (over y).
Axes of the slice: x: 2, y: 2, z: 4, core: 2. Of those that a mesh axis runs over, the one named last changes fastest.
Arguments:
- features: bfloat16 [8192, 602], P(('row', 'col')), may hold values from -6 to 6
- weight: bfloat16 [602, 256], replicated, may hold values from -0.25 to 0.25
- adj_tiles: bfloat16 [16, 2, 16, 6, 128, 128], P('row', 'col'), may hold values from 0.00077819824 to 0.03125
- tile_row: int32 [16, 2, 16, 6], P('row', 'col'), may hold values from 0 to 3, as said below
- tile_col: int32 [16, 2, 16, 6], P('row', 'col'), may hold values from 0 to 1
- tile_count: int32 [16, 2, 16], P('row', 'col'), may hold values from 1 to 6, as said below
- train_mask: int32 [8192], P(('row', 'col')), may hold values 0 or 1
- cotangent: bfloat16 [8192, 256], P(('row', 'col')), may hold values from -6 to 6
Outputs:
- hidden: bfloat16 [8192, 256], P(('row', 'col'))
- grad_features: bfloat16 [8192, 602], P(('row', 'col'))
- grad_weight: float32 [602, 256], replicated
Inputs may be any that keep to these rules, and one draw needn't show every extreme that they name: For each [r, c, j], the pairs (tile_row, tile_col) of the slots are distinct. tile_count[r, c, r] = 6 for every r and c.
All inputs are finite; a program needn't handle non-finite values. No bound on the sum of `train_mask` on one device may be relied on, other than what follows from the above.
Results may differ from a plain program's by a relative error of at most 0.0075.
Values may be sent and summed in bfloat16 or wider, within the bound.
A program may use at most 128 MiB of HBM per device.

v0:
```python
import math

import jax
import jax.numpy as jnp
from jax import lax
from jax.sharding import PartitionSpec as P


def shifted(block, axis, distance):
    devices = range(lax.axis_size(axis))
    route = [((i - distance) % len(devices), i) for i in devices]
    return lax.ppermute(block, axis, route)


def select_rows(table, one_hot):
    return jnp.einsum("kr,rah->kah", one_hot, table, preferred_element_type=jnp.float32).astype(
        jnp.bfloat16
    )


def body(features, weight, adj_tiles, tile_row, tile_col, tile_count, train_mask, cotangent):
    row_count = lax.axis_size("row")
    col_count = lax.axis_size("col")
    row_index = lax.axis_index("row")
    precise = lax.Precision.HIGHEST
    adj_blocks = adj_tiles[0, 0]
    slot_count = adj_blocks.shape[1]
    tile_size = adj_blocks.shape[2]
    nodes_dev = features.shape[0]
    block_tiles = nodes_dev // tile_size
    row_tiles = col_count * block_tiles
    projected = jnp.dot(features, weight, preferred_element_type=jnp.float32).astype(jnp.bfloat16)
    hidden_width = projected.shape[1]
    live_slots = (jnp.arange(slot_count)[None, :] < tile_count[0, 0][:, None]).astype(jnp.float32)
    row_hot = tile_row[0, 0][..., None] == jnp.arange(row_tiles)[None, None, :]
    col_hot = tile_col[0, 0][..., None] == jnp.arange(block_tiles)[None, None, :]

    def forward_part(stacked, held_block, step_block):
        picked = select_rows(
            held_block.reshape(block_tiles, tile_size, hidden_width),
            col_hot[step_block].astype(jnp.bfloat16),
        )
        product = jnp.einsum(
            "kab,kbh->kah", adj_blocks[step_block], picked, preferred_element_type=jnp.float32
        )
        return lax.dynamic_update_index_in_dim(stacked, product, step_block, 0)

    stacked = jnp.zeros((row_count, slot_count, tile_size, hidden_width), jnp.float32)

    def one_way(loop_step, carried):
        stack_now, held_block = carried
        stack_now = forward_part(stack_now, held_block, (row_index - loop_step) % row_count)
        held_block = shifted(held_block, "row", 1)
        return (stack_now, held_block)

    stacked, held_block = lax.fori_loop(0, row_count - 1, one_way, (stacked, projected))
    stacked = forward_part(stacked, held_block, (row_index - row_count + 1) % row_count)
    row_weights = row_hot.astype(jnp.float32) * live_slots[..., None]
    row_totals = jnp.einsum("jkr,jkah->rah", row_weights, stacked, precision=precise)
    pre_act = lax.psum_scatter(
        row_totals.reshape(row_tiles * tile_size, hidden_width),
        "col",
        scatter_dimension=0,
        tiled=True,
    )
    gate_value = jax.nn.sigmoid(pre_act)
    hidden = (pre_act * gate_value).astype(jnp.bfloat16)
    grad_pre = (
        cotangent.astype(jnp.float32)
        * train_mask.astype(jnp.float32)[:, None]
        * gate_value
        * (1.0 + pre_act * (1.0 - gate_value))
    ).astype(jnp.bfloat16)
    grad_rows = lax.all_gather(grad_pre, "col", axis=0, tiled=True).reshape(
        row_tiles, tile_size, hidden_width
    )

    def backward_part(step_block):
        picked = select_rows(grad_rows, row_hot[step_block].astype(jnp.bfloat16))
        product = jnp.einsum(
            "kab,kah->kbh", adj_blocks[step_block], picked, preferred_element_type=jnp.float32
        )
        weights = col_hot[step_block].astype(jnp.float32) * live_slots[step_block][:, None]
        spread = jnp.einsum("kt,kbh->tbh", weights, product, precision=precise)
        return spread.reshape(nodes_dev, hidden_width)

    def carry_on(loop_step, running):
        running = running + backward_part((row_index - 1 - loop_step) % row_count)
        return shifted(running, "row", 1)

    grad_acc = lax.fori_loop(
        0, row_count - 1, carry_on, jnp.zeros((nodes_dev, hidden_width), jnp.float32)
    )
    grad_acc = grad_acc + backward_part(row_index)
    grad_proj = grad_acc.astype(jnp.bfloat16)
    grad_scale = 1.0 / math.sqrt(row_count * col_count * nodes_dev)
    local_grad = (
        lax.dot_general(
            features, grad_proj, (((0,), (0,)), ((), ())), preferred_element_type=jnp.float32
        )
        * grad_scale
    )
    grad_weight = lax.psum(local_grad, ("row", "col"))
    grad_features = lax.dot_general(
        grad_proj, weight, (((1,), (1,)), ((), ())), preferred_element_type=jnp.float32
    ).astype(jnp.bfloat16)
    return (hidden, grad_features, grad_weight)


def solution(mesh):
    in_specs = (
        P(("row", "col"), None),
        P(),
        P("row", "col", None, None, None, None),
        P("row", "col", None, None),
        P("row", "col", None, None),
        P("row", "col", None),
        P(("row", "col")),
        P(("row", "col"), None),
    )
    out_specs = (P(("row", "col"), None), P(("row", "col"), None), P())
    return jax.shard_map(body, mesh=mesh, in_specs=in_specs, out_specs=out_specs, check_vma=False)
```

profile of v0, /device:TPU:0, one launch (start us, length us, event | category | flops | bytes accessed | tf_op | source)
XLA Modules:
  0.0 479.3 jit_solution(9794060983398271833)
XLA Ops:
  11.0 6.1 %broadcast_in_dim.25 = f32[16,6,128,256]{3,2,1,0:T(8,128)} broadcast(f32[]{:T(128)} %constant.126.clone.1), dimensions={} | broadcast | bytes 12582916 | tf_op jit(solution)/shard_map/broadcast_in_dim | solution.py:48
  17.1 108.3 %while.32 = (s32[]{:T(128)}, f32[16,6,128,256]{3,2,1,0:T(8,128)}, bf16[256,256]{1,0:T(8,128)(2,1)S(1)}, s32[]{:T(128)}, bf16[16,6,128,128]{3,2,1,0:T(8,128)(2,1)...) while((s32[]{:T(128)}, f32[16,6,128,256]{3,2,1,0:T(8,128)}, ...), condition=%wide.region_1.2_spmd, body=%wide.region_0.1_spmd.sunk | while | flops 51118096 | bytes 2688812 | solution.py:56
  17.9 2.1 fusion.86
  20.0 5.2 %collective-permute-done = bf16[256,256]{1,0:T(8,128)(2,1)S(1)} collective-permute-done((bf16[256,256]{1,0:T(8,128)(2,1)S(1)}, bf16[256,256]{1,0:T(8,128)(2,1)S(1)}, u32[]{:S(2)}, u32[]{:S(2)}) %collective-permute-start) | collective-permute-done | bytes 131104 | tf_op jit(solution)/shard_map/while/body/eval_jaxpr/ppermute | solution.py:12
  25.7 2.1 fusion.86
  27.8 4.6 collective-permute-done
  32.8 2.1 fusion.86
  34.9 4.6 collective-permute-done
  40.0 2.1 fusion.86
  42.1 4.6 collective-permute-done
  47.1 2.1 fusion.86
  49.2 4.6 collective-permute-done
  54.3 2.2 fusion.86
  56.4 4.5 collective-permute-done
  61.4 2.2 fusion.86
  63.6 4.5 collective-permute-done
  68.6 2.1 fusion.86
  70.7 4.6 collective-permute-done
  75.7 2.1 fusion.86
  77.8 4.6 collective-permute-done
  82.9 2.1 fusion.86
  85.0 4.6 collective-permute-done
  90.1 2.1 fusion.86
  92.2 4.6 collective-permute-done
  97.2 2.1 fusion.86
  99.3 4.6 collective-permute-done
  104.4 2.1 fusion.86
  106.4 4.6 collective-permute-done
  111.5 2.1 fusion.86
  113.6 4.6 collective-permute-done
  118.7 2.1 fusion.86
  120.7 4.6 collective-permute-done
  125.7 2.1 fusion.29
  127.8 18.0 %fusion.31 = f32[4,128,256]{2,0,1:T(4,128)S(1)} fusion(f32[16,6,128,256]{3,2,1,0:T(8,128)} %fusion.29, f32[16,6,4]{0,2,1:T(4,128)S(1)} %copy.18), kind=kOutput, calls=%fused_computation.38 | convolution fusion | flops 150994944 | bytes 13108736 | tf_op jit(solution)/shard_map/jkr,jkah->rah/dot_general | solution.py:59
  146.9 12.4 %reduce-scatter.2.cloned.1.call-done = f32[256,256]{1,0:T(8,128)} async-done(((f32[512,256]{1,0:T(8,128)}), f32[256,256]{1,0:T(8,128)}) %reduce-scatter.2.cloned.1.call-update) | async-done | bytes 262160 | tf_op jit(solution)/shard_map/reduce_scatter | solution.py:60
  159.2 1.8 multiply_convert_fusion
  161.0 6.1 %all_gather.3 = bf16[512,256]{1,0:T(8,128)(2,1)S(1)} all-gather(bf16[256,256]{1,0:T(8,128)(2,1)S(1)} %get-tuple-element.392), channel_id=1, replica_groups=mesh['row'=16,'col'=2] {'col'}, dimensions={0}, use_global_device_ids=true | all-gather | bytes 393216 | tf_op jit(solution)/shard_map/all_gather | solution.py:74
  168.7 1.4 fusion.34
  170.2 174.9 %while.33 = (s32[]{:T(128)}, f32[256,256]{1,0:T(8,128)S(1)}, s32[]{:T(128)}, pred[16,6,2]{1,2,0:T(4,128)(4,1)S(1)}, f32[16,6]{1,0:T(8,128)S(1)}, /*index=5*/bf16...) while((s32[]{:T(128)}, f32[256,256]{1,0:T(8,128)S(1)}, ...), condition=%wide.region_4.5_spmd, body=%wide.region_3.4_spmd.sunk | while | flops 56688668 | bytes 5441400 | solution.py:91
  171.8 1.4 fusion.95
  173.4 8.5 %collective-permute-done.1 = f32[256,256]{1,0:T(8,128)S(1)} collective-permute-done((f32[256,256]{1,0:T(8,128)S(1)}, f32[256,256]{1,0:T(8,128)S(1)}, u32[]{:S(2)}, u32[]{:S(2)}) %collective-permute-start.1) | collective-permute-done | bytes 262176 | tf_op jit(solution)/shard_map/while/body/eval_jaxpr/ppermute | solution.py:12
  185.1 8.5 %collective-permute-done.1 = f32[256,256]{1,0:T(8,128)S(1)} collective-permute-done((f32[256,256]{1,0:T(8,128)S(1)}, f32[256,256]{1,0:T(8,128)S(1)}, u32[]{:S(2)}, u32[]{:S(2)}) %collective-permute-start.1) | collective-permute-done | bytes 262176 | tf_op jit(solution)/shard_map/while/body/eval_jaxpr/ppermute | solution.py:12
  196.7 8.5 %collective-permute-done.1 = f32[256,256]{1,0:T(8,128)S(1)} collective-permute-done((f32[256,256]{1,0:T(8,128)S(1)}, f32[256,256]{1,0:T(8,128)S(1)}, u32[]{:S(2)}, u32[]{:S(2)}) %collective-permute-start.1) | collective-permute-done | bytes 262176 | tf_op jit(solution)/shard_map/while/body/eval_jaxpr/ppermute | solution.py:12
  206.8 1.4 fusion.95
  208.4 8.5 %collective-permute-done.1 = f32[256,256]{1,0:T(8,128)S(1)} collective-permute-done((f32[256,256]{1,0:T(8,128)S(1)}, f32[256,256]{1,0:T(8,128)S(1)}, u32[]{:S(2)}, u32[]{:S(2)}) %collective-permute-start.1) | collective-permute-done | bytes 262176 | tf_op jit(solution)/shard_map/while/body/eval_jaxpr/ppermute | solution.py:12
  220.0 8.5 %collective-permute-done.1 = f32[256,256]{1,0:T(8,128)S(1)} collective-permute-done((f32[256,256]{1,0:T(8,128)S(1)}, f32[256,256]{1,0:T(8,128)S(1)}, u32[]{:S(2)}, u32[]{:S(2)}) %collective-permute-start.1) | collective-permute-done | bytes 262176 | tf_op jit(solution)/shard_map/while/body/eval_jaxpr/ppermute | solution.py:12
  230.1 1.4 fusion.95
  231.7 8.5 %collective-permute-done.1 = f32[256,256]{1,0:T(8,128)S(1)} collective-permute-done((f32[256,256]{1,0:T(8,128)S(1)}, f32[256,256]{1,0:T(8,128)S(1)}, u32[]{:S(2)}, u32[]{:S(2)}) %collective-permute-start.1) | collective-permute-done | bytes 262176 | tf_op jit(solution)/shard_map/while/body/eval_jaxpr/ppermute | solution.py:12
  241.8 1.4 fusion.95
  243.4 8.5 %collective-permute-done.1 = f32[256,256]{1,0:T(8,128)S(1)} collective-permute-done((f32[256,256]{1,0:T(8,128)S(1)}, f32[256,256]{1,0:T(8,128)S(1)}, u32[]{:S(2)}, u32[]{:S(2)}) %collective-permute-start.1) | collective-permute-done | bytes 262176 | tf_op jit(solution)/shard_map/while/body/eval_jaxpr/ppermute | solution.py:12
  255.0 8.5 %collective-permute-done.1 = f32[256,256]{1,0:T(8,128)S(1)} collective-permute-done((f32[256,256]{1,0:T(8,128)S(1)}, f32[256,256]{1,0:T(8,128)S(1)}, u32[]{:S(2)}, u32[]{:S(2)}) %collective-permute-start.1) | collective-permute-done | bytes 262176 | tf_op jit(solution)/shard_map/while/body/eval_jaxpr/ppermute | solution.py:12
  265.1 1.4 fusion.95
  266.7 8.5 %collective-permute-done.1 = f32[256,256]{1,0:T(8,128)S(1)} collective-permute-done((f32[256,256]{1,0:T(8,128)S(1)}, f32[256,256]{1,0:T(8,128)S(1)}, u32[]{:S(2)}, u32[]{:S(2)}) %collective-permute-start.1) | collective-permute-done | bytes 262176 | tf_op jit(solution)/shard_map/while/body/eval_jaxpr/ppermute | solution.py:12
  278.3 8.5 %collective-permute-done.1 = f32[256,256]{1,0:T(8,128)S(1)} collective-permute-done((f32[256,256]{1,0:T(8,128)S(1)}, f32[256,256]{1,0:T(8,128)S(1)}, u32[]{:S(2)}, u32[]{:S(2)}) %collective-permute-start.1) | collective-permute-done | bytes 262176 | tf_op jit(solution)/shard_map/while/body/eval_jaxpr/ppermute | solution.py:12
  288.4 1.4 fusion.95
  290.0 8.5 %collective-permute-done.1 = f32[256,256]{1,0:T(8,128)S(1)} collective-permute-done((f32[256,256]{1,0:T(8,128)S(1)}, f32[256,256]{1,0:T(8,128)S(1)}, u32[]{:S(2)}, u32[]{:S(2)}) %collective-permute-start.1) | collective-permute-done | bytes 262176 | tf_op jit(solution)/shard_map/while/body/eval_jaxpr/ppermute | solution.py:12
  301.7 8.5 %collective-permute-done.1 = f32[256,256]{1,0:T(8,128)S(1)} collective-permute-done((f32[256,256]{1,0:T(8,128)S(1)}, f32[256,256]{1,0:T(8,128)S(1)}, u32[]{:S(2)}, u32[]{:S(2)}) %collective-permute-start.1) | collective-permute-done | bytes 262176 | tf_op jit(solution)/shard_map/while/body/eval_jaxpr/ppermute | solution.py:12
  313.3 8.5 %collective-permute-done.1 = f32[256,256]{1,0:T(8,128)S(1)} collective-permute-done((f32[256,256]{1,0:T(8,128)S(1)}, f32[256,256]{1,0:T(8,128)S(1)}, u32[]{:S(2)}, u32[]{:S(2)}) %collective-permute-start.1) | collective-permute-done | bytes 262176 | tf_op jit(solution)/shard_map/while/body/eval_jaxpr/ppermute | solution.py:12
  323.4 1.4 fusion.95
  325.0 8.5 %collective-permute-done.1 = f32[256,256]{1,0:T(8,128)S(1)} collective-permute-done((f32[256,256]{1,0:T(8,128)S(1)}, f32[256,256]{1,0:T(8,128)S(1)}, u32[]{:S(2)}, u32[]{:S(2)}) %collective-permute-start.1) | collective-permute-done | bytes 262176 | tf_op jit(solution)/shard_map/while/body/eval_jaxpr/ppermute | solution.py:12
  335.1 1.4 fusion.95
  336.6 8.5 %collective-permute-done.1 = f32[256,256]{1,0:T(8,128)S(1)} collective-permute-done((f32[256,256]{1,0:T(8,128)S(1)}, f32[256,256]{1,0:T(8,128)S(1)}, u32[]{:S(2)}, u32[]{:S(2)}) %collective-permute-start.1) | collective-permute-done | bytes 262176 | tf_op jit(solution)/shard_map/while/body/eval_jaxpr/ppermute | solution.py:12
  347.3 123.3 %all-reduce.2.cloned.1.call-done = f32[602,256]{1,0:T(8,128)} async-done(((f32[602,256]{1,0:T(8,128)}), f32[602,256]{1,0:T(8,128)}) %all-reduce.2.cloned.1.call-update) | async-done | bytes 616464 | tf_op jit(solution)/shard_map/psum | solution.py:103
  470.6 1.9 copy.89
  (173 shorter events, 51.4 us)
Async XLA Ops:
  7.2 2.5 copy-start
  7.2 152.1 %reduce-scatter.2.cloned.1.call-start = ((), (), s32[]{:S(2)}) async-start(), calls=%async_computation.1 | async-start | bytes 786432 | tf_op jit(solution)/shard_map/reduce_scatter | solution.py:60
  17.1 129.8 %copy-start.3 = (s32[256]{0:T(256)S(1)}, s32[256]{0:T(256)}, u32[]{:S(2)}) copy-start(s32[256]{0:T(256)} %param.18) | copy-start | bytes 3076
  17.1 142.2 %copy-start.2 = (bf16[256,256]{1,0:T(8,128)(2,1)S(1)}, bf16[256,256]{1,0:T(8,128)(2,1)}, u32[]{:S(2)}) copy-start(bf16[256,256]{1,0:T(8,128)(2,1)} %param.19) | copy-start | bytes 393220
  17.1 8.1 %collective-permute-start = (bf16[256,256]{1,0:T(8,128)(2,1)S(1)}, bf16[256,256]{1,0:T(8,128)(2,1)S(1)}, u32[]{:S(2)}, u32[]{:S(2)}) collective-permute-start(bf16[256,256]{1,0:T(8,128)(2,1)S(1)} %copy.77), channel_id=1, source_target_pairs={{30,0},{0,2},{2,4},{4,6},{6,8},{8,10},{10,12},{12,14},{14,16},{16,... | collective-permute-start | bytes 393224 | tf_op jit(solution)/shard_map/while/body/eval_jaxpr/ppermute | solution.py:12
  25.2 7.1 %collective-permute-start = (bf16[256,256]{1,0:T(8,128)(2,1)S(1)}, bf16[256,256]{1,0:T(8,128)(2,1)S(1)}, u32[]{:S(2)}, u32[]{:S(2)}) collective-permute-start(bf16[256,256]{1,0:T(8,128)(2,1)S(1)} %copy.77), channel_id=1, source_target_pairs={{30,0},{0,2},{2,4},{4,6},{6,8},{8,10},{10,12},{12,14},{14,16},{16,... | collective-permute-start | bytes 393224 | tf_op jit(solution)/shard_map/while/body/eval_jaxpr/ppermute | solution.py:12
  32.4 7.1 %collective-permute-start = (bf16[256,256]{1,0:T(8,128)(2,1)S(1)}, bf16[256,256]{1,0:T(8,128)(2,1)S(1)}, u32[]{:S(2)}, u32[]{:S(2)}) collective-permute-start(bf16[256,256]{1,0:T(8,128)(2,1)S(1)} %copy.77), channel_id=1, source_target_pairs={{30,0},{0,2},{2,4},{4,6},{6,8},{8,10},{10,12},{12,14},{14,16},{16,... | collective-permute-start | bytes 393224 | tf_op jit(solution)/shard_map/while/body/eval_jaxpr/ppermute | solution.py:12
  39.5 7.1 %collective-permute-start = (bf16[256,256]{1,0:T(8,128)(2,1)S(1)}, bf16[256,256]{1,0:T(8,128)(2,1)S(1)}, u32[]{:S(2)}, u32[]{:S(2)}) collective-permute-start(bf16[256,256]{1,0:T(8,128)(2,1)S(1)} %copy.77), channel_id=1, source_target_pairs={{30,0},{0,2},{2,4},{4,6},{6,8},{8,10},{10,12},{12,14},{14,16},{16,... | collective-permute-start | bytes 393224 | tf_op jit(solution)/shard_map/while/body/eval_jaxpr/ppermute | solution.py:12
  46.7 7.1 %collective-permute-start = (bf16[256,256]{1,0:T(8,128)(2,1)S(1)}, bf16[256,256]{1,0:T(8,128)(2,1)S(1)}, u32[]{:S(2)}, u32[]{:S(2)}) collective-permute-start(bf16[256,256]{1,0:T(8,128)(2,1)S(1)} %copy.77), channel_id=1, source_target_pairs={{30,0},{0,2},{2,4},{4,6},{6,8},{8,10},{10,12},{12,14},{14,16},{16,... | collective-permute-start | bytes 393224 | tf_op jit(solution)/shard_map/while/body/eval_jaxpr/ppermute | solution.py:12
  53.8 7.1 %collective-permute-start = (bf16[256,256]{1,0:T(8,128)(2,1)S(1)}, bf16[256,256]{1,0:T(8,128)(2,1)S(1)}, u32[]{:S(2)}, u32[]{:S(2)}) collective-permute-start(bf16[256,256]{1,0:T(8,128)(2,1)S(1)} %copy.77), channel_id=1, source_target_pairs={{30,0},{0,2},{2,4},{4,6},{6,8},{8,10},{10,12},{12,14},{14,16},{16,... | collective-permute-start | bytes 393224 | tf_op jit(solution)/shard_map/while/body/eval_jaxpr/ppermute | solution.py:12
  61.0 7.1 %collective-permute-start = (bf16[256,256]{1,0:T(8,128)(2,1)S(1)}, bf16[256,256]{1,0:T(8,128)(2,1)S(1)}, u32[]{:S(2)}, u32[]{:S(2)}) collective-permute-start(bf16[256,256]{1,0:T(8,128)(2,1)S(1)} %copy.77), channel_id=1, source_target_pairs={{30,0},{0,2},{2,4},{4,6},{6,8},{8,10},{10,12},{12,14},{14,16},{16,... | collective-permute-start | bytes 393224 | tf_op jit(solution)/shard_map/while/body/eval_jaxpr/ppermute | solution.py:12
  68.1 7.1 %collective-permute-start = (bf16[256,256]{1,0:T(8,128)(2,1)S(1)}, bf16[256,256]{1,0:T(8,128)(2,1)S(1)}, u32[]{:S(2)}, u32[]{:S(2)}) collective-permute-start(bf16[256,256]{1,0:T(8,128)(2,1)S(1)} %copy.77), channel_id=1, source_target_pairs={{30,0},{0,2},{2,4},{4,6},{6,8},{8,10},{10,12},{12,14},{14,16},{16,... | collective-permute-start | bytes 393224 | tf_op jit(solution)/shard_map/while/body/eval_jaxpr/ppermute | solution.py:12
  75.3 7.1 %collective-permute-start = (bf16[256,256]{1,0:T(8,128)(2,1)S(1)}, bf16[256,256]{1,0:T(8,128)(2,1)S(1)}, u32[]{:S(2)}, u32[]{:S(2)}) collective-permute-start(bf16[256,256]{1,0:T(8,128)(2,1)S(1)} %copy.77), channel_id=1, source_target_pairs={{30,0},{0,2},{2,4},{4,6},{6,8},{8,10},{10,12},{12,14},{14,16},{16,... | collective-permute-start | bytes 393224 | tf_op jit(solution)/shard_map/while/body/eval_jaxpr/ppermute | solution.py:12
  82.5 7.1 %collective-permute-start = (bf16[256,256]{1,0:T(8,128)(2,1)S(1)}, bf16[256,256]{1,0:T(8,128)(2,1)S(1)}, u32[]{:S(2)}, u32[]{:S(2)}) collective-permute-start(bf16[256,256]{1,0:T(8,128)(2,1)S(1)} %copy.77), channel_id=1, source_target_pairs={{30,0},{0,2},{2,4},{4,6},{6,8},{8,10},{10,12},{12,14},{14,16},{16,... | collective-permute-start | bytes 393224 | tf_op jit(solution)/shard_map/while/body/eval_jaxpr/ppermute | solution.py:12
  89.6 7.1 %collective-permute-start = (bf16[256,256]{1,0:T(8,128)(2,1)S(1)}, bf16[256,256]{1,0:T(8,128)(2,1)S(1)}, u32[]{:S(2)}, u32[]{:S(2)}) collective-permute-start(bf16[256,256]{1,0:T(8,128)(2,1)S(1)} %copy.77), channel_id=1, source_target_pairs={{30,0},{0,2},{2,4},{4,6},{6,8},{8,10},{10,12},{12,14},{14,16},{16,... | collective-permute-start | bytes 393224 | tf_op jit(solution)/shard_map/while/body/eval_jaxpr/ppermute | solution.py:12
  96.8 7.1 %collective-permute-start = (bf16[256,256]{1,0:T(8,128)(2,1)S(1)}, bf16[256,256]{1,0:T(8,128)(2,1)S(1)}, u32[]{:S(2)}, u32[]{:S(2)}) collective-permute-start(bf16[256,256]{1,0:T(8,128)(2,1)S(1)} %copy.77), channel_id=1, source_target_pairs={{30,0},{0,2},{2,4},{4,6},{6,8},{8,10},{10,12},{12,14},{14,16},{16,... | collective-permute-start | bytes 393224 | tf_op jit(solution)/shard_map/while/body/eval_jaxpr/ppermute | solution.py:12
  103.9 7.1 %collective-permute-start = (bf16[256,256]{1,0:T(8,128)(2,1)S(1)}, bf16[256,256]{1,0:T(8,128)(2,1)S(1)}, u32[]{:S(2)}, u32[]{:S(2)}) collective-permute-start(bf16[256,256]{1,0:T(8,128)(2,1)S(1)} %copy.77), channel_id=1, source_target_pairs={{30,0},{0,2},{2,4},{4,6},{6,8},{8,10},{10,12},{12,14},{14,16},{16,... | collective-permute-start | bytes 393224 | tf_op jit(solution)/shard_map/while/body/eval_jaxpr/ppermute | solution.py:12
  111.1 7.1 %collective-permute-start = (bf16[256,256]{1,0:T(8,128)(2,1)S(1)}, bf16[256,256]{1,0:T(8,128)(2,1)S(1)}, u32[]{:S(2)}, u32[]{:S(2)}) collective-permute-start(bf16[256,256]{1,0:T(8,128)(2,1)S(1)} %copy.77), channel_id=1, source_target_pairs={{30,0},{0,2},{2,4},{4,6},{6,8},{8,10},{10,12},{12,14},{14,16},{16,... | collective-permute-start | bytes 393224 | tf_op jit(solution)/shard_map/while/body/eval_jaxpr/ppermute | solution.py:12
  118.2 7.1 %collective-permute-start = (bf16[256,256]{1,0:T(8,128)(2,1)S(1)}, bf16[256,256]{1,0:T(8,128)(2,1)S(1)}, u32[]{:S(2)}, u32[]{:S(2)}) collective-permute-start(bf16[256,256]{1,0:T(8,128)(2,1)S(1)} %copy.77), channel_id=1, source_target_pairs={{30,0},{0,2},{2,4},{4,6},{6,8},{8,10},{10,12},{12,14},{14,16},{16,... | collective-permute-start | bytes 393224 | tf_op jit(solution)/shard_map/while/body/eval_jaxpr/ppermute | solution.py:12
  146.8 323.8 %all-reduce.2.cloned.1.call-start = ((), (), s32[]{:S(2)}) async-start(), calls=%async_computation.2 | async-start | bytes 1245184 | tf_op jit(solution)/shard_map/psum | solution.py:103
  170.2 176.1 %copy-start.1 = (bf16[602,256]{1,0:T(8,128)(2,1)S(1)}, bf16[602,256]{1,0:T(8,128)(2,1)}, u32[]{:S(2)}) copy-start(bf16[602,256]{1,0:T(8,128)(2,1)} %param.13) | copy-start | bytes 924676
  173.3 8.5 %collective-permute-start.1 = (f32[256,256]{1,0:T(8,128)S(1)}, f32[256,256]{1,0:T(8,128)S(1)}, u32[]{:S(2)}, u32[]{:S(2)}) collective-permute-start(f32[256,256]{1,0:T(8,128)S(1)} %bitcast_add_fusion.3), channel_id=1, source_target_pairs={{30,0},{0,2},{2,4},{4,6},{6,8},{8,10},{10,12},{12,14},{14,16},{16,... | collective-permute-start | bytes 786440 | tf_op jit(solution)/shard_map/while/body/eval_jaxpr/ppermute | solution.py:12
  185.0 8.5 %collective-permute-start.1 = (f32[256,256]{1,0:T(8,128)S(1)}, f32[256,256]{1,0:T(8,128)S(1)}, u32[]{:S(2)}, u32[]{:S(2)}) collective-permute-start(f32[256,256]{1,0:T(8,128)S(1)} %bitcast_add_fusion.3), channel_id=1, source_target_pairs={{30,0},{0,2},{2,4},{4,6},{6,8},{8,10},{10,12},{12,14},{14,16},{16,... | collective-permute-start | bytes 786440 | tf_op jit(solution)/shard_map/while/body/eval_jaxpr/ppermute | solution.py:12
  196.7 8.5 %collective-permute-start.1 = (f32[256,256]{1,0:T(8,128)S(1)}, f32[256,256]{1,0:T(8,128)S(1)}, u32[]{:S(2)}, u32[]{:S(2)}) collective-permute-start(f32[256,256]{1,0:T(8,128)S(1)} %bitcast_add_fusion.3), channel_id=1, source_target_pairs={{30,0},{0,2},{2,4},{4,6},{6,8},{8,10},{10,12},{12,14},{14,16},{16,... | collective-permute-start | bytes 786440 | tf_op jit(solution)/shard_map/while/body/eval_jaxpr/ppermute | solution.py:12
  208.3 8.5 %collective-permute-start.1 = (f32[256,256]{1,0:T(8,128)S(1)}, f32[256,256]{1,0:T(8,128)S(1)}, u32[]{:S(2)}, u32[]{:S(2)}) collective-permute-start(f32[256,256]{1,0:T(8,128)S(1)} %bitcast_add_fusion.3), channel_id=1, source_target_pairs={{30,0},{0,2},{2,4},{4,6},{6,8},{8,10},{10,12},{12,14},{14,16},{16,... | collective-permute-start | bytes 786440 | tf_op jit(solution)/shard_map/while/body/eval_jaxpr/ppermute | solution.py:12
  220.0 8.5 %collective-permute-start.1 = (f32[256,256]{1,0:T(8,128)S(1)}, f32[256,256]{1,0:T(8,128)S(1)}, u32[]{:S(2)}, u32[]{:S(2)}) collective-permute-start(f32[256,256]{1,0:T(8,128)S(1)} %bitcast_add_fusion.3), channel_id=1, source_target_pairs={{30,0},{0,2},{2,4},{4,6},{6,8},{8,10},{10,12},{12,14},{14,16},{16,... | collective-permute-start | bytes 786440 | tf_op jit(solution)/shard_map/while/body/eval_jaxpr/ppermute | solution.py:12
  231.6 8.5 %collective-permute-start.1 = (f32[256,256]{1,0:T(8,128)S(1)}, f32[256,256]{1,0:T(8,128)S(1)}, u32[]{:S(2)}, u32[]{:S(2)}) collective-permute-start(f32[256,256]{1,0:T(8,128)S(1)} %bitcast_add_fusion.3), channel_id=1, source_target_pairs={{30,0},{0,2},{2,4},{4,6},{6,8},{8,10},{10,12},{12,14},{14,16},{16,... | collective-permute-start | bytes 786440 | tf_op jit(solution)/shard_map/while/body/eval_jaxpr/ppermute | solution.py:12
  243.3 8.5 %collective-permute-start.1 = (f32[256,256]{1,0:T(8,128)S(1)}, f32[256,256]{1,0:T(8,128)S(1)}, u32[]{:S(2)}, u32[]{:S(2)}) collective-permute-start(f32[256,256]{1,0:T(8,128)S(1)} %bitcast_add_fusion.3), channel_id=1, source_target_pairs={{30,0},{0,2},{2,4},{4,6},{6,8},{8,10},{10,12},{12,14},{14,16},{16,... | collective-permute-start | bytes 786440 | tf_op jit(solution)/shard_map/while/body/eval_jaxpr/ppermute | solution.py:12
  255.0 8.5 %collective-permute-start.1 = (f32[256,256]{1,0:T(8,128)S(1)}, f32[256,256]{1,0:T(8,128)S(1)}, u32[]{:S(2)}, u32[]{:S(2)}) collective-permute-start(f32[256,256]{1,0:T(8,128)S(1)} %bitcast_add_fusion.3), channel_id=1, source_target_pairs={{30,0},{0,2},{2,4},{4,6},{6,8},{8,10},{10,12},{12,14},{14,16},{16,... | collective-permute-start | bytes 786440 | tf_op jit(solution)/shard_map/while/body/eval_jaxpr/ppermute | solution.py:12
  266.6 8.5 %collective-permute-start.1 = (f32[256,256]{1,0:T(8,128)S(1)}, f32[256,256]{1,0:T(8,128)S(1)}, u32[]{:S(2)}, u32[]{:S(2)}) collective-permute-start(f32[256,256]{1,0:T(8,128)S(1)} %bitcast_add_fusion.3), channel_id=1, source_target_pairs={{30,0},{0,2},{2,4},{4,6},{6,8},{8,10},{10,12},{12,14},{14,16},{16,... | collective-permute-start | bytes 786440 | tf_op jit(solution)/shard_map/while/body/eval_jaxpr/ppermute | solution.py:12
  278.3 8.5 %collective-permute-start.1 = (f32[256,256]{1,0:T(8,128)S(1)}, f32[256,256]{1,0:T(8,128)S(1)}, u32[]{:S(2)}, u32[]{:S(2)}) collective-permute-start(f32[256,256]{1,0:T(8,128)S(1)} %bitcast_add_fusion.3), channel_id=1, source_target_pairs={{30,0},{0,2},{2,4},{4,6},{6,8},{8,10},{10,12},{12,14},{14,16},{16,... | collective-permute-start | bytes 786440 | tf_op jit(solution)/shard_map/while/body/eval_jaxpr/ppermute | solution.py:12
  289.9 8.5 %collective-permute-start.1 = (f32[256,256]{1,0:T(8,128)S(1)}, f32[256,256]{1,0:T(8,128)S(1)}, u32[]{:S(2)}, u32[]{:S(2)}) collective-permute-start(f32[256,256]{1,0:T(8,128)S(1)} %bitcast_add_fusion.3), channel_id=1, source_target_pairs={{30,0},{0,2},{2,4},{4,6},{6,8},{8,10},{10,12},{12,14},{14,16},{16,... | collective-permute-start | bytes 786440 | tf_op jit(solution)/shard_map/while/body/eval_jaxpr/ppermute | solution.py:12
  301.6 8.5 %collective-permute-start.1 = (f32[256,256]{1,0:T(8,128)S(1)}, f32[256,256]{1,0:T(8,128)S(1)}, u32[]{:S(2)}, u32[]{:S(2)}) collective-permute-start(f32[256,256]{1,0:T(8,128)S(1)} %bitcast_add_fusion.3), channel_id=1, source_target_pairs={{30,0},{0,2},{2,4},{4,6},{6,8},{8,10},{10,12},{12,14},{14,16},{16,... | collective-permute-start | bytes 786440 | tf_op jit(solution)/shard_map/while/body/eval_jaxpr/ppermute | solution.py:12
  313.3 8.5 %collective-permute-start.1 = (f32[256,256]{1,0:T(8,128)S(1)}, f32[256,256]{1,0:T(8,128)S(1)}, u32[]{:S(2)}, u32[]{:S(2)}) collective-permute-start(f32[256,256]{1,0:T(8,128)S(1)} %bitcast_add_fusion.3), channel_id=1, source_target_pairs={{30,0},{0,2},{2,4},{4,6},{6,8},{8,10},{10,12},{12,14},{14,16},{16,... | collective-permute-start | bytes 786440 | tf_op jit(solution)/shard_map/while/body/eval_jaxpr/ppermute | solution.py:12
  324.9 8.5 %collective-permute-start.1 = (f32[256,256]{1,0:T(8,128)S(1)}, f32[256,256]{1,0:T(8,128)S(1)}, u32[]{:S(2)}, u32[]{:S(2)}) collective-permute-start(f32[256,256]{1,0:T(8,128)S(1)} %bitcast_add_fusion.3), channel_id=1, source_target_pairs={{30,0},{0,2},{2,4},{4,6},{6,8},{8,10},{10,12},{12,14},{14,16},{16,... | collective-permute-start | bytes 786440 | tf_op jit(solution)/shard_map/while/body/eval_jaxpr/ppermute | solution.py:12
  336.6 8.5 %collective-permute-start.1 = (f32[256,256]{1,0:T(8,128)S(1)}, f32[256,256]{1,0:T(8,128)S(1)}, u32[]{:S(2)}, u32[]{:S(2)}) collective-permute-start(f32[256,256]{1,0:T(8,128)S(1)} %bitcast_add_fusion.3), channel_id=1, source_target_pairs={{30,0},{0,2},{2,4},{4,6},{6,8},{8,10},{10,12},{12,14},{14,16},{16,... | collective-permute-start | bytes 786440 | tf_op jit(solution)/shard_map/while/body/eval_jaxpr/ppermute | solution.py:12
Sparse Core Ops, SparseCore 0:
  146.9 12.3 reduce-scatter.1
  346.4 124.1 all-reduce.1
where the time goes:
time: 480 us; the launch traced here: 479 us
  waiting for transfers between devices  332 us (69%)
  matrix products  109 us (23%)
  between operations  14.2 us (3%)
  local copies, waits for them, and re-layouts  11.2 us (2%)
  blocking collectives  6.08 us (1%)
    ppermute x30, waiting for transfers between devices, shifted(): return lax.ppermute(block, axis, route)  197 us
    psum x1, waiting for transfers between devices, body(): grad_weight = lax.psum(local_grad, ('row', 'col'))  123 us
    dot_general x16, matrix products, forward_part(): jnp.einsum('kab,kbh->kah', adj_blocks[step_block], picked, preferred_elem...  33.5 us
    dot_general x16, matrix products, backward_part(): spread = jnp.einsum('kt,kbh->tbh', weights, product, precision=precise)  22.6 us
    dot_general x16, matrix products, backward_part(): jnp.einsum('kab,kah->kbh', adj_blocks[step_block], picked, preferred_elem...  19.9 us
    dot_general x1, matrix products, body(): jnp.einsum('jkr,jkah->rah', row_weights, stacked, precision=precise)  18 us
    reduce_scatter x1, waiting for transfers between devices, body(): lax.psum_scatter(row_totals.reshape(row_tiles * tile_size, hidden_width),...  12.4 us
    dot_general x32, matrix products, select_rows(): jnp.einsum('kr,rah->kah', one_hot, table, preferred_element_type=jnp.floa...  11.4 us
  transfers between devices with their start and end apart: 32, of which 32 were waited for; matrix products, arithmetic and copies ran while one was open for 8% of the time, Pallas kernels for 0%

commit v1 on v0

v1 whole, which is shorter than its diff:
```python
import functools
import math

import jax
import jax.numpy as jnp
from jax import lax
from jax.experimental import pallas as pl
from jax.experimental.pallas import tpu as pltpu
from jax.sharding import PartitionSpec as P

BF16 = jnp.bfloat16
F32 = jnp.float32


def layer_kernel(
    row_count,
    col_count,
    grad_scale,
    trow_ref,
    tcol_ref,
    tcount_ref,
    adj_ref,
    feat_ref,
    weight_ref,
    mask_ref,
    cot_ref,
    hidden_ref,
    gfeat_ref,
    gweight_ref,
    tiles,
    dense,
    held,
    acc,
    col_out,
    col_in,
    grad_t,
    core_out,
    core_in,
    mate_out,
    mate_in,
    line_out,
    line_in,
    feat_pad,
    gw_loc,
    gw_s1,
    gw_r1,
    gw_s2,
    gw_r2,
    gw_line,
    gw_full,
    adj_sem,
    g_line,
    g_mate,
    g_core,
    g_recv,
    c_send,
    c_recv,
    t_send,
    t_recv,
    b_core_send,
    b_core_recv,
    b_mate_send,
    b_mate_recv,
    b_line_send,
    b_line_recv,
    w_send,
    w_recv,
    w_plane_send,
    w_plane_recv,
    w_line_send,
    w_line_recv,
    w_gat_send,
    w_gat_recv,
):
    line_count = row_count // 4
    me = lax.axis_index("row")
    col = lax.axis_index("col")
    core = me % 2
    mate = (me // 2) % 2
    line = me // 4
    slot_count = adj_ref.shape[3]
    tile = adj_ref.shape[4]
    nodes = feat_ref.shape[1]
    block_tiles = nodes // tile

    def row_id(l, m, k):
        return (l * 2 + m) * 2 + k

    def line_at(d):
        return (line + d) % line_count

    to_core = {"row": row_id(line, mate, 1 - core)}
    to_mate = {"row": row_id(line, 1 - mate, core)}

    def to_line(d):
        return {"row": row_id(line_at(d), mate, core)}

    def to_col(d):
        return {"col": (col + d) % col_count}

    plane = [(dm, dc) for dm in range(2) for dc in range(col_count) if dm + dc > 0]

    def plane_part(dm, dc):
        return ((mate + dm) % 2) * col_count + (col + dc) % col_count

    def to_plane(dm, dc):
        return {
            "row": row_id(line, (mate + dm) % 2, core),
            "col": (col + dc) % col_count,
        }

    near = sorted(range(1, line_count), key=lambda d: min(d, line_count - d))
    far = near[::-1]
    peers = [to_core, to_mate] + [to_line(d) for d in near]
    peers += [to_col(d) for d in range(1, col_count)]
    peers += [to_plane(1, dc) for dc in range(1, col_count)]

    started = []

    def push(src, dst, send, recv, target):
        copy = pltpu.make_async_remote_copy(
            src_ref=src,
            dst_ref=dst,
            send_sem=send,
            recv_sem=recv,
            device_id=target,
            device_id_type=pl.DeviceIdType.MESH,
        )
        copy.start()
        started.append(copy)

    def arrived(dst, recv):
        pltpu.make_async_remote_copy(
            src_ref=dst,
            dst_ref=dst,
            send_sem=recv,
            recv_sem=recv,
            device_id=to_core,
            device_id_type=pl.DeviceIdType.MESH,
        ).wait_recv()

    adj_copy = pltpu.make_async_copy(
        adj_ref.at[0, 0], tiles.at[:, pl.ds(0, slot_count)], adj_sem
    )
    adj_copy.start()
    barrier = pltpu.get_barrier_semaphore()
    for peer in peers:
        pl.semaphore_signal(
            barrier, inc=1, device_id=peer, device_id_type=pl.DeviceIdType.MESH
        )
    held[me] = lax.dot_general(
        feat_ref[...], weight_ref[...], (((0,), (0,)), ((), ())), preferred_element_type=F32
    ).astype(BF16)
    pl.semaphore_wait(barrier, len(peers))

    own = held.at[me]
    for d in near:
        push(own, own, g_line.at[d], g_recv.at[me], to_line(d))
    push(own, own, g_mate.at[line], g_recv.at[me], to_mate)
    push(own, own, g_core.at[line * 2 + mate], g_recv.at[me], to_core)

    tiles[:, slot_count] = jnp.zeros_like(tiles[:, slot_count])
    adj_copy.wait()

    def build(j, carry):
        filled = []
        for s in range(slot_count):
            live = s < tcount_ref[0, 0, j]
            place = trow_ref[0, 0, s, j] * block_tiles + tcol_ref[0, 0, s, j]
            filled.append(jnp.where(live, place, -1))
        for r in range(col_count * block_tiles):
            for t in range(block_tiles):
                slot = jnp.int32(slot_count)
                for s in range(slot_count):
                    slot = jnp.where(filled[s] == r * block_tiles + t, s, slot)
                dense[
                    j,
                    r // block_tiles,
                    pl.ds((r % block_tiles) * tile, tile),
                    pl.ds(t * tile, tile),
                ] = tiles[j, slot]
        return carry

    lax.fori_loop(0, row_count, build, 0)

    def accumulate(j, first=False):
        def one(i, carry):
            product = jnp.dot(dense[j, i], held[j], preferred_element_type=F32)
            acc[i] = product if first else acc[i] + product
            return carry

        lax.fori_loop(0, col_count, one, 0, unroll=col_count <= 2)

    def forward_mate(l):
        block = row_id(l, mate, core)
        push(held.at[block], held.at[block], g_mate.at[l], g_recv.at[block], to_mate)

    def forward_core(l, m):
        block = row_id(l, m, core)
        push(held.at[block], held.at[block], g_core.at[l * 2 + m], g_recv.at[block], to_core)

    def take(l, m, k):
        block = row_id(l, m, k)
        arrived(held.at[block], g_recv.at[block])
        return block

    accumulate(me, first=True)
    accumulate(take(line, mate, 1 - core))
    late = []
    last_line = line
    for d in near:
        l = line_at(d)
        block = take(l, mate, core)
        forward_mate(l)
        forward_core(l, mate)
        crossed = take(last_line, 1 - mate, core)
        forward_core(last_line, 1 - mate)
        for item in late:
            accumulate(take(*item))
        accumulate(block)
        accumulate(crossed)
        late = [(l, mate, 1 - core), (last_line, 1 - mate, 1 - core)]
        last_line = l
    for item in late:
        accumulate(take(*item))
    crossed = take(last_line, 1 - mate, core)
    forward_core(last_line, 1 - mate)
    accumulate(crossed)
    accumulate(take(last_line, 1 - mate, 1 - core))

    for d in range(1, col_count):
        col_out[d] = acc[(col + d) % col_count].astype(BF16)
        push(col_out.at[d], col_in.at[d], c_send.at[d], c_recv.at[d], to_col(d))
    width = feat_ref.shape[0]
    pad_from = (width // 16) * 16
    feat_pad[pad_from:, :] = jnp.zeros_like(feat_pad[pad_from:, :])
    feat_pad[:width, :] = feat_ref[...]
    pre_act = acc[col]
    for d in range(1, col_count):
        arrived(col_in.at[d], c_recv.at[d])
        pre_act = pre_act + col_in[d].astype(F32)

    gate = jax.nn.sigmoid(pre_act)
    grad_pre = cot_ref[...].astype(F32) * gate * (1.0 + pre_act * (1.0 - gate))
    grad_t[col] = (grad_pre.T * mask_ref[...].astype(F32)).astype(BF16)
    for d in range(1, col_count):
        push(grad_t.at[col], grad_t.at[col], t_send.at[d], t_recv.at[col], to_col(d))
    hidden_ref[...] = (pre_act * gate).astype(BF16)
    for d in range(1, col_count):
        other = (col + d) % col_count
        arrived(grad_t.at[other], t_recv.at[other])

    def partial_sum(block):
        def one(i, running):
            return running + jnp.dot(grad_t[i], dense[block, i], preferred_element_type=F32)

        start = jnp.dot(grad_t[0], dense[block, 0], preferred_element_type=F32)
        return lax.fori_loop(1, col_count, one, start, unroll=col_count <= 2)

    order = far + [0]

    def send_core(side):
        for d in order:
            l = line_at(d)
            at = l * 2 + side
            core_out[at] = partial_sum(row_id(l, side, 1 - core)).astype(BF16)
            push(core_out.at[at], core_in.at[at], b_core_send.at[at], b_core_recv.at[at], to_core)

    send_core(1 - mate)
    for d in order:
        l = line_at(d)
        at = l * 2 + 1 - mate
        mine = partial_sum(row_id(l, 1 - mate, core))
        arrived(core_in.at[at], b_core_recv.at[at])
        mate_out[l] = (mine + core_in[at].astype(F32)).astype(BF16)
        push(mate_out.at[l], mate_in.at[l], b_mate_send.at[l], b_mate_recv.at[l], to_mate)
    send_core(mate)
    total = None
    for d in order:
        l = line_at(d)
        at = l * 2 + mate
        mine = partial_sum(row_id(l, mate, core))
        arrived(core_in.at[at], b_core_recv.at[at])
        mine = mine + core_in[at].astype(F32)
        arrived(mate_in.at[l], b_mate_recv.at[l])
        mine = mine + mate_in[l].astype(F32)
        if d:
            line_out[d] = mine.astype(BF16)
            push(line_out.at[d], line_in.at[d], b_line_send.at[d], b_line_recv.at[d], to_line(d))
        else:
            total = mine
    for d in far:
        arrived(line_in.at[d], b_line_recv.at[d])
        total = total + line_in[d].astype(F32)

    wire = gw_full.dtype
    proj_t = total.astype(BF16)
    local = lax.dot_general(
        proj_t, feat_pad[...], (((1,), (1,)), ((), ())), preferred_element_type=F32
    )
    gw_loc[...] = (local * grad_scale).reshape(gw_loc.shape)
    gw_s1[...] = gw_loc[1 - core].astype(wire)
    push(gw_s1, gw_r1, w_send.at[0], w_recv.at[0], to_core)
    gfeat_ref[...] = jnp.dot(weight_ref[...], proj_t, preferred_element_type=F32).astype(BF16)
    arrived(gw_r1, w_recv.at[0])
    for dm, dc in plane[::-1]:
        at = dm * col_count + dc
        p = plane_part(dm, dc)
        gw_s2[at] = (gw_loc[core, p] + gw_r1[p].astype(F32)).astype(wire)
        push(gw_s2.at[at], gw_r2.at[at], w_plane_send.at[at], w_plane_recv.at[at], to_plane(dm, dc))
    own_part = plane_part(0, 0)
    part = gw_loc[core, own_part] + gw_r1[own_part].astype(F32)
    for dm, dc in plane:
        at = dm * col_count + dc
        arrived(gw_r2.at[at], w_plane_recv.at[at])
        part = part + gw_r2[at].astype(F32)
    gw_line[line] = part.astype(wire)
    for d in far:
        push(gw_line.at[line], gw_line.at[line], w_line_send.at[d], w_line_recv.at[line], to_line(d))
    for d in near:
        l = line_at(d)
        arrived(gw_line.at[l], w_line_recv.at[l])
    part = gw_line[0].astype(F32)
    for i in range(1, line_count):
        part = part + gw_line[i].astype(F32)
    gw_full[core, own_part] = part.astype(wire)
    mine = gw_full.at[core, own_part]
    for dm, dc in plane[::-1]:
        at = dm * col_count + dc
        push(mine, mine, w_gat_send.at[at], w_gat_recv.at[own_part], to_plane(dm, dc))
    for dm, dc in plane:
        p = plane_part(dm, dc)
        arrived(gw_full.at[core, p], w_gat_recv.at[p])
    mine = gw_full.at[core]
    push(mine, mine, w_send.at[1], w_recv.at[1], to_core)
    arrived(gw_full.at[1 - core], w_recv.at[1])
    gweight_ref[...] = gw_full[...].reshape(gweight_ref.shape[1], gweight_ref.shape[0]).T

    for copy in started:
        copy.wait_send()


def body(features, weight, adj_tiles, tile_row, tile_col, tile_count, train_mask, cotangent):
    rows = lax.axis_size("row")
    cols = lax.axis_size("col")
    slot_count, tile = adj_tiles.shape[3], adj_tiles.shape[4]
    nodes, width = features.shape
    hid = weight.shape[1]
    lines = rows // 4
    padded = -(-width // 128) * 128
    parts = 2 * cols
    piece = hid // (2 * parts)
    wire = BF16 if piece % 16 == 0 else F32
    grad_scale = 1.0 / math.sqrt(rows * cols * nodes)

    vmem = pltpu.VMEM
    sems = lambda n: pltpu.SemaphoreType.DMA((n,))
    scratch = [
        vmem((rows, slot_count + 1, tile, tile), BF16),
        vmem((rows, cols, nodes, nodes), BF16),
        vmem((rows, nodes, hid), BF16),
        vmem((cols, nodes, hid), F32),
        vmem((cols, nodes, hid), BF16),
        vmem((cols, nodes, hid), BF16),
        vmem((cols, hid, nodes), BF16),
        vmem((rows // 2, hid, nodes), BF16),
        vmem((rows // 2, hid, nodes), BF16),
        vmem((lines, hid, nodes), BF16),
        vmem((lines, hid, nodes), BF16),
        vmem((lines, hid, nodes), BF16),
        vmem((lines, hid, nodes), BF16),
        vmem((padded, nodes), BF16),
        vmem((2, parts, piece, padded), F32),
        vmem((parts, piece, padded), wire),
        vmem((parts, piece, padded), wire),
        vmem((parts, piece, padded), wire),
        vmem((parts, piece, padded), wire),
        vmem((lines, piece, padded), wire),
        vmem((2, parts, piece, padded), wire),
        pltpu.SemaphoreType.DMA,
        sems(lines),
        sems(lines),
        sems(rows // 2),
        sems(rows),
        sems(cols),
        sems(cols),
        sems(cols),
        sems(cols),
        sems(rows // 2),
        sems(rows // 2),
        sems(lines),
        sems(lines),
        sems(lines),
        sems(lines),
        sems(2),
        sems(2),
        sems(parts),
        sems(parts),
        sems(lines),
        sems(lines),
        sems(parts),
        sems(parts),
    ]
    whole = pl.BlockSpec(memory_space=pltpu.VMEM)
    hidden, grad_features, grad_weight = pl.pallas_call(
        functools.partial(layer_kernel, rows, cols, grad_scale),
        out_shape=(
            jax.ShapeDtypeStruct((nodes, hid), BF16),
            jax.ShapeDtypeStruct((width, nodes), BF16),
            jax.ShapeDtypeStruct((padded, hid), wire),
        ),
        in_specs=[
            pl.BlockSpec(memory_space=pltpu.SMEM),
            pl.BlockSpec(memory_space=pltpu.SMEM),
            pl.BlockSpec(memory_space=pltpu.SMEM),
            pl.BlockSpec(memory_space=pl.ANY),
            whole,
            whole,
            whole,
            whole,
        ],
        out_specs=(whole, whole, whole),
        scratch_shapes=scratch,
        compiler_params=pltpu.CompilerParams(
            collective_id=0, has_side_effects=True, vmem_limit_bytes=63 * 1024 * 1024
        ),
        name="graph_layer",
    )(
        tile_row.swapaxes(2, 3),
        tile_col.swapaxes(2, 3),
        tile_count,
        adj_tiles,
        features.T,
        weight,
        train_mask.reshape(1, nodes),
        cotangent,
    )
    return (hidden, grad_features.T, grad_weight[:width].astype(F32))


def solution(mesh):
    in_specs = (
        P(("row", "col"), None),
        P(),
        P("row", "col", None, None, None, None),
        P("row", "col", None, None),
        P("row", "col", None, None),
        P("row", "col", None),
        P(("row", "col")),
        P(("row", "col"), None),
    )
    out_specs = (P(("row", "col"), None), P(("row", "col"), None), P())
    return jax.shard_map(body, mesh=mesh, in_specs=in_specs, out_specs=out_specs, check_vma=False)
```

time: 480 us -> 78.9 us (0.16)
  waiting for transfers between devices: 332 us -> 0 us
  matrix products: 109 us -> 0 us
  Pallas kernels: 0 us -> 71.5 us
  between operations: 14.2 us -> 0.64 us
  local copies, waits for them, and re-layouts: 11.2 us -> 4.57 us
  blocking collectives: 6.08 us -> 0 us
    ppermute x30 -> x0, waiting for transfers between devices: 197 us -> none  [shifted(): return lax.ppermute(block, axis, route)]
    psum x1 -> x0, waiting for transfers between devices: 123 us -> none  [body(): grad_weight = lax.psum(local_grad, ('row', 'col'))]
    dot_general x84 -> x0, matrix products: 109 us -> none  [the longest x16 33.5 us: forward_part(): jnp.einsum('kab,kbh->kah', adj_blocks[step_block], picked, preferred_elem...]
    pallas_call x0 -> x1, Pallas kernels: none -> 71.5 us  [body(): pl.pallas_call(functools.partial(layer_kernel, rows, cols, grad_scale), o...]
    reduce_scatter x1 -> x0, waiting for transfers between devices: 12.4 us -> none  [body(): lax.psum_scatter(row_totals.reshape(row_tiles * tile_size, hidden_width),...]
    broadcast_in_dim x2 -> x0, local copies, waits for them, and re-layouts: 6.11 us -> none  [the longest x1 6.09 us: body(): jnp.zeros((row_count, slot_count, tile_size, hidden_width), jnp.float32)]
    all_gather x1 -> x0, blocking collectives: 6.08 us -> none  [body(): lax.all_gather(grad_pre, 'col', axis=0, tiled=True)]
  transfers between devices with their start and end apart: 32 -> 0, of which waited for: 32 -> 0; matrix products, arithmetic and copies ran while one was open for 8% -> 0% of each run, Pallas kernels for 0% -> 0%
where the time goes in v1:
time: 78.9 us; the launch traced here: 78.5 us
  Pallas kernels  71.5 us (91%)
  local copies, waits for them, and re-layouts  4.57 us (6%)
  other arithmetic  1.83 us (2%)
    pallas_call x1, Pallas kernels, body(): pl.pallas_call(functools.partial(layer_kernel, rows, cols, grad_scale), o...  71.5 us
    unnamed x2, local copies, waits for them, and re-layouts  3.27 us
    convert_element_type x1, other arithmetic, body(): return (hidden, grad_features.T, grad_weight[:width].astype(F32))  1.83 us

profile of v1, /device:TPU:0, one launch (start us, length us, event | category | flops | bytes accessed | tf_op | source)
XLA Modules:
  0.0 78.5 jit_solution(17949321042669023181)
XLA Ops:
  0.6 1.3 %copy_bitcast_fusion = (s32[1,1,6,16]{3,2,1,0:T(8,128)}, s32[1,1,6,16]{3,2,1,0:T(8,128)}) fusion(s32[1,1,16,6]{2,1,3,0:T(1,128)} %param.12, s32[1,1,16,6]{2,1,3,0:T(1,128)} %param.11), kind=kLoop, calls=%fused_computation.1 | loop fusion | bytes 1536 | tf_op jit(solution)/shard_map/transpose | solution.py:430
  1.9 71.5 %graph_layer.1 = (bf16[256,256]{1,0:T(8,128)(2,1)}, bf16[602,256]{1,0:T(8,128)(2,1)}, bf16[640,256]{1,0:T(8,128)(2,1)}) custom-call(s32[1,1,6,16]{3,2,1,0:T(8,128)} %get-tuple-element.10.trow_ref, s32[1,1,6,16]{3,2,1,0:T(8,128)} %get-tuple-element.9.tcol_ref, s32[1,1,16]{2,1,0:T(1,128)} %tcount_ref.1, bf16[1,1,16,6,128,128]{5,4,3,2,1,0:T(8,128)(2,1)} %adj_ref.1, ...), custom_call_target="tpu_custom_call" | custom-call | tf_op jit(solution)/shard_map/graph_layer/pallas_call | solution.py:405
  73.4 1.8 %slice_convert_fusion = f32[602,256]{1,0:T(8,128)} fusion(bf16[640,256]{1,0:T(8,128)(2,1)} %get-tuple-element.8), kind=kLoop, calls=%fused_computation | loop fusion | flops 154112 | bytes 924672 | tf_op jit(solution)/shard_map/convert_element_type | solution.py:438
  75.3 1.6 %copy.17 = bf16[256,256]{1,0:T(8,128)(2,1)} copy(bf16[256,256]{1,0:T(8,128)(2,1)} %get-tuple-element.14) | data formatting | bytes 262144
  76.8 1.7 %copy.18 = bf16[256,602]{0,1:T(8,128)(2,1)} copy(bf16[256,602]{0,1:T(8,128)(2,1)} %bitcast.8) | data formatting | bytes 616448

commit v2 on v1

v2 whole, which is shorter than its diff:
```python
import functools
import math

import jax
import jax.numpy as jnp
from jax import lax
from jax.experimental import pallas as pl
from jax.experimental.pallas import tpu as pltpu
from jax.sharding import PartitionSpec as P

BF16 = jnp.bfloat16
F32 = jnp.float32


def layer_kernel(
    row_count,
    col_count,
    grad_scale,
    halves,
    trow_ref,
    tcol_ref,
    tcount_ref,
    adj_ref,
    feat_ref,
    weight_ref,
    mask_ref,
    cot_ref,
    hidden_ref,
    gfeat_ref,
    gweight_ref,
    tiles,
    dense,
    held,
    acc,
    col_out,
    col_in,
    grad_t,
    grad_cat,
    core_out,
    core_in,
    mate_out,
    mate_in,
    line_out,
    line_in,
    own_sum,
    proj_t,
    feat_pad,
    gw_loc,
    gw_s1,
    gw_r1,
    gw_s2,
    gw_r2,
    gw_line,
    gw_full,
    adj_sem,
    g_line,
    g_mate,
    g_core,
    g_recv,
    c_send,
    c_recv,
    t_send,
    t_recv,
    b_core_send,
    b_core_recv,
    b_mate_send,
    b_mate_recv,
    b_line_send,
    b_line_recv,
    w_send,
    w_recv,
    w_plane_send,
    w_plane_recv,
    w_line_send,
    w_line_recv,
    w_gat_send,
    w_gat_recv,
):
    line_count = row_count // 4
    me = lax.axis_index("row")
    col = lax.axis_index("col")
    core = me % 2
    mate = (me // 2) % 2
    line = me // 4
    slot_count = adj_ref.shape[3]
    tile = adj_ref.shape[4]
    nodes = feat_ref.shape[1]
    block_tiles = nodes // tile
    hid = weight_ref.shape[1] // halves

    def row_id(l, m, k):
        return (l * 2 + m) * 2 + k

    def line_at(d):
        return (line + d) % line_count

    to_core = {"row": row_id(line, mate, 1 - core)}
    to_mate = {"row": row_id(line, 1 - mate, core)}

    def to_line(d):
        return {"row": row_id(line_at(d), mate, core)}

    def to_col(d):
        return {"col": (col + d) % col_count}

    plane = [(dm, dc) for dm in range(2) for dc in range(col_count) if dm + dc > 0]

    def plane_part(dm, dc):
        return ((mate + dm) % 2) * col_count + (col + dc) % col_count

    def to_plane(dm, dc):
        return {
            "row": row_id(line, (mate + dm) % 2, core),
            "col": (col + dc) % col_count,
        }

    near = sorted(range(1, line_count), key=lambda d: min(d, line_count - d))
    far = near[::-1]
    peers = [to_core, to_mate] + [to_line(d) for d in near]
    peers += [to_col(d) for d in range(1, col_count)]
    peers += [to_plane(1, dc) for dc in range(1, col_count)]

    started = []

    def push(src, dst, send, recv, target):
        copy = pltpu.make_async_remote_copy(
            src_ref=src,
            dst_ref=dst,
            send_sem=send,
            recv_sem=recv,
            device_id=target,
            device_id_type=pl.DeviceIdType.MESH,
        )
        copy.start()
        started.append(copy)

    def arrived(dst, recv):
        pltpu.make_async_remote_copy(
            src_ref=dst,
            dst_ref=dst,
            send_sem=recv,
            recv_sem=recv,
            device_id=to_core,
            device_id_type=pl.DeviceIdType.MESH,
        ).wait_recv()

    adj_copy = pltpu.make_async_copy(
        adj_ref.at[0, 0], tiles.at[:, pl.ds(0, slot_count)], adj_sem
    )
    adj_copy.start()
    barrier = pltpu.get_barrier_semaphore()
    for peer in peers:
        pl.semaphore_signal(
            barrier, inc=1, device_id=peer, device_id_type=pl.DeviceIdType.MESH
        )
    projected = lax.dot_general(
        feat_ref[...], weight_ref[...], (((0,), (0,)), ((), ())), preferred_element_type=F32
    ).astype(BF16)
    for h in range(halves):
        held[h, me] = projected[:, h * hid : (h + 1) * hid]
    pl.semaphore_wait(barrier, len(peers))

    def send_own(h):
        own = held.at[h, me]
        for d in near:
            push(own, own, g_line.at[h, d], g_recv.at[h, me], to_line(d))
        push(own, own, g_mate.at[h, line], g_recv.at[h, me], to_mate)
        push(own, own, g_core.at[h, line * 2 + mate], g_recv.at[h, me], to_core)

    send_own(0)
    tiles[:, slot_count] = jnp.zeros_like(tiles[:, slot_count])
    adj_copy.wait()

    def build(j, carry):
        filled = []
        for s in range(slot_count):
            live = s < tcount_ref[0, 0, j]
            place = trow_ref[0, s, 0, j] * block_tiles + tcol_ref[0, s, 0, j]
            filled.append(jnp.where(live, place, -1))
        for r in range(col_count * block_tiles):
            for t in range(block_tiles):
                slot = jnp.int32(slot_count)
                for s in range(slot_count):
                    slot = jnp.where(filled[s] == r * block_tiles + t, s, slot)
                dense[j, pl.ds(r * tile, tile), pl.ds(t * tile, tile)] = tiles[j, slot]
        return carry

    if halves == 1:
        lax.fori_loop(0, row_count, build, 0)

    def rows_of(i):
        return pl.ds(pl.multiple_of(i * nodes, nodes), nodes)

    def accumulate(h, j, first=False):
        if halves > 1 and h == 0:
            build(j, 0)
        if col_count <= 2:
            product = jnp.dot(dense[j], held[h, j], preferred_element_type=F32)
            acc[h] = product if first else acc[h] + product
            return

        def one(i, carry):
            product = jnp.dot(dense[j, rows_of(i)], held[h, j], preferred_element_type=F32)
            acc[h, rows_of(i)] = product if first else acc[h, rows_of(i)] + product
            return carry

        lax.fori_loop(0, col_count, one, 0)

    def forward_mate(h, l):
        block = row_id(l, mate, core)
        ref = held.at[h, block]
        push(ref, ref, g_mate.at[h, l], g_recv.at[h, block], to_mate)

    def forward_core(h, l, m):
        block = row_id(l, m, core)
        ref = held.at[h, block]
        push(ref, ref, g_core.at[h, l * 2 + m], g_recv.at[h, block], to_core)

    def take(h, l, m, k):
        block = row_id(l, m, k)
        arrived(held.at[h, block], g_recv.at[h, block])
        return block

    def gather_steps(h):
        accumulate(h, me, first=True)
        if h + 1 < halves:
            send_own(h + 1)
        accumulate(h, take(h, line, mate, 1 - core))
        late = []
        last_line = line
        for d in near:
            l = line_at(d)
            block = take(h, l, mate, core)
            forward_mate(h, l)
            forward_core(h, l, mate)
            crossed = take(h, last_line, 1 - mate, core)
            forward_core(h, last_line, 1 - mate)
            for item in late:
                accumulate(h, take(h, *item))
            accumulate(h, block)
            accumulate(h, crossed)
            late = [(l, mate, 1 - core), (last_line, 1 - mate, 1 - core)]
            last_line = l
            yield
        for item in late:
            accumulate(h, take(h, *item))
        crossed = take(h, last_line, 1 - mate, core)
        forward_core(h, last_line, 1 - mate)
        accumulate(h, crossed)
        accumulate(h, take(h, last_line, 1 - mate, 1 - core))

    def col_send(h):
        for d in range(1, col_count):
            col_out[h, d] = acc[h, rows_of((col + d) % col_count)].astype(BF16)
            push(col_out.at[h, d], col_in.at[h, d], c_send.at[h, d], c_recv.at[h, d], to_col(d))

    def col_finish(h):
        lanes = slice(h * hid, (h + 1) * hid)
        pre_act = acc[h, rows_of(col)]
        for d in range(1, col_count):
            arrived(col_in.at[h, d], c_recv.at[h, d])
            pre_act = pre_act + col_in[h, d].astype(F32)
        gate = jax.nn.sigmoid(pre_act)
        grad_pre = cot_ref[:, lanes].astype(F32) * gate * (1.0 + pre_act * (1.0 - gate))
        grad_t[h, col] = (grad_pre.T * mask_ref[...].astype(F32)).astype(BF16)
        mine = grad_t.at[h, col]
        for d in range(1, col_count):
            push(mine, mine, t_send.at[h, d], t_recv.at[h, col], to_col(d))
        hidden_ref[:, lanes] = (pre_act * gate).astype(BF16)

    def col_take(h):
        for d in range(1, col_count):
            other = (col + d) % col_count
            arrived(grad_t.at[h, other], t_recv.at[h, other])
        for i in range(col_count):
            grad_cat[h, :, i * nodes : (i + 1) * nodes] = grad_t[h, i]

    def partial_sum(h, block):
        if col_count <= 2:
            return jnp.dot(grad_cat[h], dense[block], preferred_element_type=F32)

        def one(i, running):
            return running + jnp.dot(
                grad_t[h, i], dense[block, rows_of(i)], preferred_element_type=F32
            )

        return lax.fori_loop(0, col_count, one, jnp.zeros((hid, nodes), F32))

    order = far + [0]

    def send_core(h, side):
        for d in order:
            l = line_at(d)
            at = l * 2 + side
            core_out[h, at] = partial_sum(h, row_id(l, side, 1 - core)).astype(BF16)
            push(
                core_out.at[h, at],
                core_in.at[h, at],
                b_core_send.at[h, at],
                b_core_recv.at[h, at],
                to_core,
            )

    def send_mate(h):
        for d in order:
            l = line_at(d)
            at = l * 2 + 1 - mate
            mine = partial_sum(h, row_id(l, 1 - mate, core))
            arrived(core_in.at[h, at], b_core_recv.at[h, at])
            mate_out[h, l] = (mine + core_in[h, at].astype(F32)).astype(BF16)
            push(
                mate_out.at[h, l],
                mate_in.at[h, l],
                b_mate_send.at[h, l],
                b_mate_recv.at[h, l],
                to_mate,
            )

    def send_line(h):
        for d in order:
            l = line_at(d)
            at = l * 2 + mate
            mine = partial_sum(h, row_id(l, mate, core))
            arrived(core_in.at[h, at], b_core_recv.at[h, at])
            mine = mine + core_in[h, at].astype(F32)
            arrived(mate_in.at[h, l], b_mate_recv.at[h, l])
            mine = mine + mate_in[h, l].astype(F32)
            if d:
                line_out[h, d] = mine.astype(BF16)
                push(
                    line_out.at[h, d],
                    line_in.at[h, d],
                    b_line_send.at[h, d],
                    b_line_recv.at[h, d],
                    to_line(d),
                )
            else:
                own_sum[h] = mine

    def finish(h):
        total = own_sum[h]
        for d in far:
            arrived(line_in.at[h, d], b_line_recv.at[h, d])
            total = total + line_in[h, d].astype(F32)
        proj_t[h * hid : (h + 1) * hid, :] = total.astype(BF16)

    def pad_features():
        width = feat_ref.shape[0]
        pad_from = (width // 16) * 16
        feat_pad[pad_from:, :] = jnp.zeros_like(feat_pad[pad_from:, :])
        feat_pad[:width, :] = feat_ref[...]

    wire = gw_full.dtype

    def weight_steps(h):
        local = lax.dot_general(
            proj_t[h * hid : (h + 1) * hid, :],
            feat_pad[...],
            (((1,), (1,)), ((), ())),
            preferred_element_type=F32,
        )
        gw_loc[h] = (local * grad_scale).reshape(gw_loc.shape[1:])
        gw_s1[h] = gw_loc[h, 1 - core].astype(wire)
        push(gw_s1.at[h], gw_r1.at[h], w_send.at[h, 0], w_recv.at[h, 0], to_core)
        yield
        arrived(gw_r1.at[h], w_recv.at[h, 0])
        for dm, dc in plane[::-1]:
            at = dm * col_count + dc
            p = plane_part(dm, dc)
            gw_s2[h, at] = (gw_loc[h, core, p] + gw_r1[h, p].astype(F32)).astype(wire)
            push(
                gw_s2.at[h, at],
                gw_r2.at[h, at],
                w_plane_send.at[h, at],
                w_plane_recv.at[h, at],
                to_plane(dm, dc),
            )
        own_part = plane_part(0, 0)
        part = gw_loc[h, core, own_part] + gw_r1[h, own_part].astype(F32)
        yield
        for dm, dc in plane:
            at = dm * col_count + dc
            arrived(gw_r2.at[h, at], w_plane_recv.at[h, at])
            part = part + gw_r2[h, at].astype(F32)
        gw_line[h, line] = part.astype(wire)
        mine = gw_line.at[h, line]
        for d in far:
            push(mine, mine, w_line_send.at[h, d], w_line_recv.at[h, line], to_line(d))
        yield
        for d in near:
            l = line_at(d)
            arrived(gw_line.at[h, l], w_line_recv.at[h, l])
        part = gw_line[h, 0].astype(F32)
        for i in range(1, line_count):
            part = part + gw_line[h, i].astype(F32)
        gw_full[h, core, own_part] = part.astype(wire)
        mine = gw_full.at[h, core, own_part]
        for dm, dc in plane[::-1]:
            at = dm * col_count + dc
            push(
                mine,
                mine,
                w_gat_send.at[h, at],
                w_gat_recv.at[h, own_part],
                to_plane(dm, dc),
            )
        yield
        for dm, dc in plane:
            p = plane_part(dm, dc)
            arrived(gw_full.at[h, core, p], w_gat_recv.at[h, p])
        mine = gw_full.at[h, core]
        push(mine, mine, w_send.at[h, 1], w_recv.at[h, 1], to_core)
        yield
        arrived(gw_full.at[h, 1 - core], w_recv.at[h, 1])
        full = gw_full[h].reshape(hid, gweight_ref.shape[0])
        gweight_ref[:, h * hid : (h + 1) * hid] = full.T

    def feature_gradient():
        gfeat_ref[...] = jnp.dot(
            weight_ref[...], proj_t[...], preferred_element_type=F32
        ).astype(BF16)

    if halves == 2:
        first, second = gather_steps(0), gather_steps(1)
        for _ in near:
            next(first)
        next(second)
        for _ in first:
            pass
        col_send(0)
        next(second)
        pad_features()
        col_finish(0)
        for _ in second:
            pass
        col_send(1)
        col_take(0)
        send_core(0, 1 - mate)
        col_finish(1)
        send_mate(0)
        send_core(0, mate)
        col_take(1)
        send_core(1, 1 - mate)
        send_line(0)
        send_mate(1)
        send_core(1, mate)
        send_line(1)
        finish(0)
        ahead, behind = weight_steps(0), weight_steps(1)
        next(ahead)
        next(ahead)
        finish(1)
        next(behind)
        for _ in ahead:
            next(behind)
        feature_gradient()
        for _ in behind:
            pass
    else:
        for _ in gather_steps(0):
            pass
        col_send(0)
        pad_features()
        col_finish(0)
        col_take(0)
        send_core(0, 1 - mate)
        send_mate(0)
        send_core(0, mate)
        send_line(0)
        finish(0)
        steps = weight_steps(0)
        next(steps)
        feature_gradient()
        for _ in steps:
            pass

    for copy in started:
        copy.wait_send()


def results_kernel(hidden_in, gfeat_in, gweight_in, hidden_ref, gfeat_ref, gweight_ref):
    hidden_ref[...] = hidden_in[...]
    gfeat_ref[...] = gfeat_in[...]
    gweight_ref[...] = gweight_in[: gweight_ref.shape[0], :].astype(F32)


def body(features, weight, adj_tiles, tile_row, tile_col, tile_count, train_mask, cotangent):
    rows = lax.axis_size("row")
    cols = lax.axis_size("col")
    slot_count, tile = adj_tiles.shape[3], adj_tiles.shape[4]
    nodes, width = features.shape
    hid = weight.shape[1]
    lines = rows // 4
    padded = -(-width // 128) * 128
    parts = 2 * cols
    halves = 2 if hid % (32 * parts) == 0 else 1
    part_hid = hid // halves
    piece = part_hid // (2 * parts)
    wire = BF16 if piece % 16 == 0 else F32
    grad_scale = 1.0 / math.sqrt(rows * cols * nodes)

    vmem = pltpu.VMEM
    half_sems = lambda n: pltpu.SemaphoreType.DMA((halves, n))
    scratch = [
        vmem((rows, slot_count + 1, tile, tile), BF16),
        vmem((rows, cols * nodes, nodes), BF16),
        vmem((halves, rows, nodes, part_hid), BF16),
        vmem((halves, cols * nodes, part_hid), F32),
        vmem((halves, cols, nodes, part_hid), BF16),
        vmem((halves, cols, nodes, part_hid), BF16),
        vmem((halves, cols, part_hid, nodes), BF16),
        vmem((halves, part_hid, cols * nodes), BF16),
        vmem((halves, rows // 2, part_hid, nodes), BF16),
        vmem((halves, rows // 2, part_hid, nodes), BF16),
        vmem((halves, lines, part_hid, nodes), BF16),
        vmem((halves, lines, part_hid, nodes), BF16),
        vmem((halves, lines, part_hid, nodes), BF16),
        vmem((halves, lines, part_hid, nodes), BF16),
        vmem((halves, part_hid, nodes), F32),
        vmem((hid, nodes), BF16),
        vmem((padded, nodes), BF16),
        vmem((halves, 2, parts, piece, padded), F32),
        vmem((halves, parts, piece, padded), wire),
        vmem((halves, parts, piece, padded), wire),
        vmem((halves, parts, piece, padded), wire),
        vmem((halves, parts, piece, padded), wire),
        vmem((halves, lines, piece, padded), wire),
        vmem((halves, 2, parts, piece, padded), wire),
        pltpu.SemaphoreType.DMA,
        half_sems(lines),
        half_sems(lines),
        half_sems(rows // 2),
        half_sems(rows),
        half_sems(cols),
        half_sems(cols),
        half_sems(cols),
        half_sems(cols),
        half_sems(rows // 2),
        half_sems(rows // 2),
        half_sems(lines),
        half_sems(lines),
        half_sems(lines),
        half_sems(lines),
        half_sems(2),
        half_sems(2),
        half_sems(parts),
        half_sems(parts),
        half_sems(lines),
        half_sems(lines),
        half_sems(parts),
        half_sems(parts),
    ]
    whole = pl.BlockSpec(memory_space=pltpu.VMEM)
    hidden, grad_features, grad_weight = pl.pallas_call(
        functools.partial(layer_kernel, rows, cols, grad_scale, halves),
        out_shape=(
            jax.ShapeDtypeStruct((nodes, hid), BF16),
            jax.ShapeDtypeStruct((width, nodes), BF16),
            jax.ShapeDtypeStruct((padded, hid), wire),
        ),
        in_specs=[
            pl.BlockSpec(memory_space=pltpu.SMEM),
            pl.BlockSpec(memory_space=pltpu.SMEM),
            pl.BlockSpec(memory_space=pltpu.SMEM),
            pl.BlockSpec(memory_space=pl.ANY),
            whole,
            whole,
            whole,
            whole,
        ],
        out_specs=(whole, whole, whole),
        scratch_shapes=scratch,
        compiler_params=pltpu.CompilerParams(
            collective_id=0, has_side_effects=True, vmem_limit_bytes=63 * 1024 * 1024
        ),
        name="graph_layer",
    )(
        tile_row.transpose(0, 3, 1, 2),
        tile_col.transpose(0, 3, 1, 2),
        tile_count,
        adj_tiles,
        features.T,
        weight,
        train_mask.reshape(1, nodes),
        cotangent,
    )
    hidden, grad_features, grad_weight = pl.pallas_call(
        results_kernel,
        out_shape=(
            jax.ShapeDtypeStruct((nodes, hid), BF16),
            jax.ShapeDtypeStruct((width, nodes), BF16),
            jax.ShapeDtypeStruct((width, hid), F32),
        ),
        in_specs=[whole] * 3,
        out_specs=(whole, whole, whole),
        name="results",
    )(hidden, grad_features, grad_weight)
    return (hidden, grad_features.T, grad_weight)


def solution(mesh):
    in_specs = (
        P(("row", "col"), None),
        P(),
        P("row", "col", None, None, None, None),
        P("row", "col", None, None),
        P("row", "col", None, None),
        P("row", "col", None),
        P(("row", "col")),
        P(("row", "col"), None),
    )
    out_specs = (P(("row", "col"), None), P(("row", "col"), None), P())
    return jax.shard_map(body, mesh=mesh, in_specs=in_specs, out_specs=out_specs, check_vma=False)
```

time: 78.9 us -> 70.7 us (0.90)
  local copies, waits for them, and re-layouts: 4.57 us -> 0 us
  other arithmetic: 1.83 us -> 0 us
  Pallas kernels: 71.5 us -> 69.7 us
    unnamed x2 -> x0, local copies, waits for them, and re-layouts: 3.27 us -> none
    convert_element_type x1 -> x0, other arithmetic: 1.83 us -> none  [body(): return (hidden, grad_features.T, grad_weight[:width].astype(F32))]
    pallas_call x1 -> x2, Pallas kernels: 71.5 us -> 69.7 us  [the longest x1 67.6 us: body(): pl.pallas_call(functools.partial(layer_kernel, rows, cols, grad_scale, ha...]
    transpose x1 -> x0, local copies, waits for them, and re-layouts: 1.3 us -> none  [body(): tile_col.swapaxes(2, 3)]
where the time goes in v2:
time: 70.7 us; the launch traced here: 70.4 us
  Pallas kernels  69.7 us (99%)
    pallas_call x1, Pallas kernels, body(): pl.pallas_call(functools.partial(layer_kernel, rows, cols, grad_scale, ha...  67.6 us
    pallas_call x1, Pallas kernels, body(): pl.pallas_call(results_kernel, out_shape=(jax.ShapeDtypeStruct((nodes, hi...  2.12 us

profile of v2, /device:TPU:0, one launch (start us, length us, event | category | flops | bytes accessed | tf_op | source)
XLA Modules:
  0.0 70.4 jit_solution(6624160870536351779)
XLA Ops:
  0.6 67.6 %graph_layer.1 = (bf16[256,256]{1,0:T(8,128)(2,1)}, bf16[602,256]{1,0:T(8,128)(2,1)}, bf16[640,256]{1,0:T(8,128)(2,1)}) custom-call(s32[1,6,1,16]{3,2,1,0:T(1,128)} %bitcast.6, s32[1,6,1,16]{3,2,1,0:T(1,128)} %bitcast.7, s32[1,1,16]{2,1,0:T(1,128)} %tcount_ref.1, bf16[1,1,16,6,128,128]{5,4,3,2,1,0:T(8,128)(2,1)} %adj_ref.1, bf16[602,256]{1,0:T(8,128)(2,1)} %bitcast.5, ...), custom_call_target="tpu_custom_call" | custom-call | tf_op jit(solution)/shard_map/graph_layer/pallas_call | solution.py:554
  68.2 2.1 %results.1 = (bf16[256,256]{1,0:T(8,128)(2,1)}, bf16[602,256]{1,0:T(8,128)(2,1)}, f32[602,256]{1,0:T(8,128)}) custom-call(bf16[256,256]{1,0:T(8,128)(2,1)} %get-tuple-element.9.hidden_in, bf16[602,256]{1,0:T(8,128)(2,1)} %get-tuple-element.10.gfeat_in, bf16[640,256]{1,0:T(8,128)(2,1)} %get-tuple-element.11.gweight_in), custom_call_target="tpu_custom_call" | custom-call | tf_op jit(solution)/shard_map/results/pallas_call | solution.py:587

commit v3 on v2

--- a/solution.py
+++ b/solution.py
@@ -46,8 +46,6 @@
     proj_t,
     feat_pad,
     gw_loc,
-    gw_s1,
-    gw_r1,
     gw_s2,
     gw_r2,
     gw_line,
@@ -67,8 +65,6 @@
     b_mate_recv,
     b_line_send,
     b_line_recv,
-    w_send,
-    w_recv,
     w_plane_send,
     w_plane_recv,
     w_line_send,
@@ -103,22 +99,25 @@
     def to_col(d):
         return {"col": (col + d) % col_count}
 
-    plane = [(dm, dc) for dm in range(2) for dc in range(col_count) if dm + dc > 0]
-
-    def plane_part(dm, dc):
-        return ((mate + dm) % 2) * col_count + (col + dc) % col_count
-
-    def to_plane(dm, dc):
+    plane = [
+        (dk, dm, dc) for dk in range(2) for dm in range(2) for dc in range(col_count)
+    ][1:]
+
+    def plane_offset(dk, dm, dc):
+        return (dk * 2 + dm) * col_count + dc
+
+    def plane_part(dk, dm, dc):
+        return plane_offset((core + dk) % 2, (mate + dm) % 2, (col + dc) % col_count)
+
+    def to_plane(dk, dm, dc):
         return {
-            "row": row_id(line, (mate + dm) % 2, core),
+            "row": row_id(line, (mate + dm) % 2, (core + dk) % 2),
             "col": (col + dc) % col_count,
         }
 
     near = sorted(range(1, line_count), key=lambda d: min(d, line_count - d))
     far = near[::-1]
-    peers = [to_core, to_mate] + [to_line(d) for d in near]
-    peers += [to_col(d) for d in range(1, col_count)]
-    peers += [to_plane(1, dc) for dc in range(1, col_count)]
+    peers = [to_plane(*step) for step in plane] + [to_line(d) for d in near]
 
     started = []
 
@@ -360,26 +359,21 @@
             preferred_element_type=F32,
         )
         gw_loc[h] = (local * grad_scale).reshape(gw_loc.shape[1:])
-        gw_s1[h] = gw_loc[h, 1 - core].astype(wire)
-        push(gw_s1.at[h], gw_r1.at[h], w_send.at[h, 0], w_recv.at[h, 0], to_core)
-        yield
-        arrived(gw_r1.at[h], w_recv.at[h, 0])
-        for dm, dc in plane[::-1]:
-            at = dm * col_count + dc
-            p = plane_part(dm, dc)
-            gw_s2[h, at] = (gw_loc[h, core, p] + gw_r1[h, p].astype(F32)).astype(wire)
+        for step in plane[::-1]:
+            at = plane_offset(*step)
+            gw_s2[h, at] = gw_loc[h, plane_part(*step)].astype(wire)
             push(
                 gw_s2.at[h, at],
                 gw_r2.at[h, at],
                 w_plane_send.at[h, at],
                 w_plane_recv.at[h, at],
-                to_plane(dm, dc),
+                to_plane(*step),
             )
-        own_part = plane_part(0, 0)
-        part = gw_loc[h, core, own_part] + gw_r1[h, own_part].astype(F32)
+        own_part = plane_part(0, 0, 0)
+        part = gw_loc[h, own_part]
         yield
-        for dm, dc in plane:
-            at = dm * col_count + dc
+        for step in plane:
+            at = plane_offset(*step)
             arrived(gw_r2.at[h, at], w_plane_recv.at[h, at])
             part = part + gw_r2[h, at].astype(F32)
         gw_line[h, line] = part.astype(wire)
@@ -393,25 +387,20 @@
         part = gw_line[h, 0].astype(F32)
         for i in range(1, line_count):
             part = part + gw_line[h, i].astype(F32)
-        gw_full[h, core, own_part] = part.astype(wire)
-        mine = gw_full.at[h, core, own_part]
-        for dm, dc in plane[::-1]:
-            at = dm * col_count + dc
+        gw_full[h, own_part] = part.astype(wire)
+        mine = gw_full.at[h, own_part]
+        for step in plane[::-1]:
             push(
                 mine,
                 mine,
-                w_gat_send.at[h, at],
+                w_gat_send.at[h, plane_offset(*step)],
                 w_gat_recv.at[h, own_part],
-                to_plane(dm, dc),
+                to_plane(*step),
             )
         yield
-        for dm, dc in plane:
-            p = plane_part(dm, dc)
-            arrived(gw_full.at[h, core, p], w_gat_recv.at[h, p])
-        mine = gw_full.at[h, core]
-        push(mine, mine, w_send.at[h, 1], w_recv.at[h, 1], to_core)
-        yield
-        arrived(gw_full.at[h, 1 - core], w_recv.at[h, 1])
+        for step in plane:
+            p = plane_part(*step)
+            arrived(gw_full.at[h, p], w_gat_recv.at[h, p])
         full = gw_full[h].reshape(hid, gweight_ref.shape[0])
         gweight_ref[:, h * hid : (h + 1) * hid] = full.T
 
@@ -448,7 +437,6 @@
         finish(0)
         ahead, behind = weight_steps(0), weight_steps(1)
         next(ahead)
-        next(ahead)
         finish(1)
         next(behind)
         for _ in ahead:
@@ -492,10 +480,10 @@
     hid = weight.shape[1]
     lines = rows // 4
     padded = -(-width // 128) * 128
-    parts = 2 * cols
-    halves = 2 if hid % (32 * parts) == 0 else 1
+    parts = 4 * cols
+    halves = 2 if hid % (16 * parts) == 0 and cols <= 2 else 1
     part_hid = hid // halves
-    piece = part_hid // (2 * parts)
+    piece = part_hid // parts
     wire = BF16 if piece % 16 == 0 else F32
     grad_scale = 1.0 / math.sqrt(rows * cols * nodes)
 
@@ -519,13 +507,11 @@
         vmem((halves, part_hid, nodes), F32),
         vmem((hid, nodes), BF16),
         vmem((padded, nodes), BF16),
-        vmem((halves, 2, parts, piece, padded), F32),
-        vmem((halves, parts, piece, padded), wire),
-        vmem((halves, parts, piece, padded), wire),
+        vmem((halves, parts, piece, padded), F32),
         vmem((halves, parts, piece, padded), wire),
         vmem((halves, parts, piece, padded), wire),
         vmem((halves, lines, piece, padded), wire),
-        vmem((halves, 2, parts, piece, padded), wire),
+        vmem((halves, parts, piece, padded), wire),
         pltpu.SemaphoreType.DMA,
         half_sems(lines),
         half_sems(lines),
@@ -541,8 +527,6 @@
         half_sems(lines),
         half_sems(lines),
         half_sems(lines),
-        half_sems(2),
-        half_sems(2),
         half_sems(parts),
         half_sems(parts),
         half_sems(lines),

time: 70.7 us -> 68.4 us (0.967)
  Pallas kernels: 69.7 us -> 67.6 us
    pallas_call x1, Pallas kernels: 67.6 us -> 65.5 us  [body(): pl.pallas_call(functools.partial(layer_kernel, rows, cols, grad_scale, ha...]
where the time goes in v3:
time: 68.4 us; the launch traced here: 68.2 us
  Pallas kernels  67.6 us (99%)
    pallas_call x1, Pallas kernels, body(): pl.pallas_call(functools.partial(layer_kernel, rows, cols, grad_scale, ha...  65.5 us
    pallas_call x1, Pallas kernels, body(): pl.pallas_call(results_kernel, out_shape=(jax.ShapeDtypeStruct((nodes, hi...  2.12 us

profile of v3, /device:TPU:0, one launch (start us, length us, event | category | flops | bytes accessed | tf_op | source)
XLA Modules:
  0.0 68.2 jit_solution(11486969409551252720)
XLA Ops:
  0.6 65.5 %graph_layer.1 = (bf16[256,256]{1,0:T(8,128)(2,1)}, bf16[602,256]{1,0:T(8,128)(2,1)}, bf16[640,256]{1,0:T(8,128)(2,1)}) custom-call(s32[1,6,1,16]{3,2,1,0:T(1,128)} %bitcast.6, s32[1,6,1,16]{3,2,1,0:T(1,128)} %bitcast.7, s32[1,1,16]{2,1,0:T(1,128)} %tcount_ref.1, bf16[1,1,16,6,128,128]{5,4,3,2,1,0:T(8,128)(2,1)} %adj_ref.1, bf16[602,256]{1,0:T(8,128)(2,1)} %bitcast.5, ...), custom_call_target="tpu_custom_call" | custom-call | tf_op jit(solution)/shard_map/graph_layer/pallas_call | solution.py:538
  66.1 2.1 %results.1 = (bf16[256,256]{1,0:T(8,128)(2,1)}, bf16[602,256]{1,0:T(8,128)(2,1)}, f32[602,256]{1,0:T(8,128)}) custom-call(bf16[256,256]{1,0:T(8,128)(2,1)} %get-tuple-element.9.hidden_in, bf16[602,256]{1,0:T(8,128)(2,1)} %get-tuple-element.10.gfeat_in, bf16[640,256]{1,0:T(8,128)(2,1)} %get-tuple-element.11.gweight_in), custom_call_target="tpu_custom_call" | custom-call | tf_op jit(solution)/shard_map/results/pallas_call | solution.py:571
